TPU v7x, 32 devices: a whole 2x2x4 slice. The times are simulated.
32 devices in a mesh: lat: 8 (over y, x, core), lon: 4 (over z).
Axes of the slice: x: 2, y: 2, z: 4, core: 2. Of those that a mesh axis runs over, the one named last changes fastest.
Arguments:
- grid_state: bfloat16 [120, 192, 128], P('lat', 'lon'), may hold values from -6 to 6
- weight_in: bfloat16 [6, 128, 384], replicated, may hold values from -0.5 to 0.5
- bias_in: float32 [6, 384], replicated, may hold values from -4 to 4
- weight_out: bfloat16 [6, 384, 128], replicated, may hold values from -0.3125 to 0.3125
- quad_weights: float32 [120], replicated, may hold values from 0.5 to 2
- diffusion: float32 [128], replicated, may hold values from 0.3 to 30
- legendre: bfloat16 [32, 120, 32], P('lon'), may hold values from -0.5 to 0.5
- chan_table: int32 [128], replicated, may hold values from 0 to 127, each once
- wave_table: int32 [32], replicated, may hold values from 0 to 31, each once
Outputs:
- updated: bfloat16 [120, 192, 128], P('lat', 'lon')
- spectral: float32 [32, 128, 2, 32], P('lon', 'lat')
Inputs may be any that keep to these rules, and one draw needn't show every extreme that they name: `chan_table`: each channel 0 to 127 stands exactly once. `wave_table`: each wavenumber 0 to 31 stands exactly once.
All inputs are finite; a program needn't handle non-finite values.
Results may differ from a plain program's by a relative error of at most 0.012.
Values may be sent and summed in bfloat16 or wider, within the bound.
A program may use at most 64 MiB of HBM per device.

v0:
```python
import math
import jax
import jax.numpy as jnp
from jax import lax
from jax.sharding import PartitionSpec as P


def column_layers(column_rows, weight_in, bias_in, weight_out):
    hidden_state = column_rows.astype(jnp.float32)
    for layer_idx in range(weight_in.shape[0]):
        inv_rms = lax.rsqrt(jnp.mean(hidden_state * hidden_state, axis=-1, keepdims=True) + 1e-06)
        normed = (hidden_state * inv_rms).astype(jnp.bfloat16)
        pre_act = (
            jnp.dot(normed, weight_in[layer_idx], preferred_element_type=jnp.float32)
            + bias_in[layer_idx]
        )
        activation = jax.nn.gelu(pre_act, approximate=True).astype(jnp.bfloat16)
        hidden_state = hidden_state + jnp.dot(
            activation, weight_out[layer_idx], preferred_element_type=jnp.float32
        )
    return hidden_state.astype(jnp.bfloat16)


def trig_table(wave_ids, longitudes, lon_total):
    phase_angle = (wave_ids[:, None] * longitudes[None, :] % lon_total).astype(jnp.float32) * (
        2.0 * math.pi / lon_total
    )
    stacked = jnp.stack([jnp.cos(phase_angle), -jnp.sin(phase_angle)], axis=1) / math.sqrt(
        lon_total
    )
    return stacked.astype(jnp.bfloat16)


def pick_channels(rows, chosen):
    picked = jnp.einsum("ljc,ck->ljk", rows, chosen, preferred_element_type=jnp.float32)
    return picked.astype(jnp.bfloat16)


def local(
    grid_state,
    weight_in,
    bias_in,
    weight_out,
    quad_weights,
    diffusion,
    legendre,
    chan_table,
    wave_table,
):
    lat_rows, lon_cols, channels = grid_state.shape
    lat_count = lax.axis_size("lat")
    lon_count = lax.axis_size("lon")
    lon_total = lon_cols * lon_count
    per_dev = channels // lat_count
    owned_slots = legendre.shape[0]
    top_degree = legendre.shape[2]
    flat_rows = grid_state.reshape(lat_rows * lon_cols, channels)
    columns = column_layers(flat_rows, weight_in, bias_in, weight_out).reshape(
        lat_rows, lon_cols, channels
    )
    every = jnp.arange(channels, dtype=jnp.int32)
    chosen = (every[:, None] == chan_table[None, :]).astype(jnp.bfloat16)
    ordered = pick_channels(columns, chosen)
    levels = lax.all_to_all(ordered, "lat", split_axis=2, concat_axis=0, tiled=True)
    trig_all = trig_table(wave_table, jnp.arange(lon_total, dtype=jnp.int32), lon_total)
    lon_here = lax.axis_index("lon") * lon_cols + jnp.arange(lon_cols, dtype=jnp.int32)
    trig_rows = trig_table(wave_table, lon_here, lon_total)
    fourier = lax.psum_scatter(
        jnp.einsum("srj,ljk->skrl", trig_rows, levels, preferred_element_type=jnp.float32),
        "lon",
        scatter_dimension=0,
        tiled=True,
    )
    weighted = (fourier * quad_weights).astype(jnp.bfloat16)
    raw_spec = jnp.einsum("skrl,sln->skrn", weighted, legendre, preferred_element_type=jnp.float32)
    my_waves = lax.dynamic_slice_in_dim(
        wave_table, lax.axis_index("lon") * owned_slots, owned_slots, 0
    )
    degree = jnp.arange(top_degree, dtype=jnp.int32)
    triangle = (degree[None, :] >= my_waves[:, None]).astype(jnp.float32)
    my_chans = lax.dynamic_slice_in_dim(chan_table, lax.axis_index("lat") * per_dev, per_dev, 0)
    degree_f = degree.astype(jnp.float32)
    damping = (
        jnp.sum(jnp.where(my_chans[:, None] == every[None, :], diffusion[None, :], 0.0), 1)[:, None]
        * (degree_f * (degree_f + 1.0))[None, :]
        / float(top_degree * top_degree)
    )
    spectral = raw_spec * triangle[:, None, None, :] / (1.0 + damping)[None, :, None, :]
    back_fourier = jnp.einsum(
        "skrn,sln->skrl",
        spectral.astype(jnp.bfloat16),
        legendre,
        preferred_element_type=jnp.float32,
    ).astype(jnp.bfloat16)
    all_waves = lax.all_to_all(back_fourier, "lon", split_axis=3, concat_axis=0, tiled=True)
    band_tendency = jnp.einsum(
        "skrl,srj->ljk", all_waves, trig_all, preferred_element_type=jnp.float32
    ).astype(jnp.bfloat16)
    tendency = lax.all_to_all(
        lax.all_to_all(band_tendency, "lon", split_axis=1, concat_axis=0, tiled=True),
        "lat",
        split_axis=0,
        concat_axis=2,
        tiled=True,
    )
    tendency = pick_channels(tendency, chosen.T)
    updated = (columns.astype(jnp.float32) + tendency.astype(jnp.float32)).astype(jnp.bfloat16)
    return (updated, spectral)


def solution(mesh):
    placed = (P("lat", "lon", None), P(), P(), P(), P(), P(), P("lon", None, None), P(), P())
    return jax.shard_map(
        local,
        mesh=mesh,
        in_specs=placed,
        out_specs=(P("lat", "lon", None), P("lon", "lat", None, None)),
        check_vma=False,
    )
```

profile of v0, /device:TPU:0, one launch (start us, length us, event | category | flops | bytes accessed | tf_op | source)
XLA Modules:
  0.0 100.8 jit_solution(6014327949595269104)
XLA Ops:
  7.2 1.1 %multiply_reduce_fusion.5 = f32[15,48]{1,0:T(8,128)S(1)} fusion(bf16[15,48,128]{2,1,0:T(8,128)(2,1)} %param.9), kind=kLoop, calls=%fused_computation.121 | loop fusion | flops 275760 | bytes 187200 | tf_op jit(solution)/shard_map/reduce_sum | solution.py:11
  8.3 1.0 slice_reduce_fusion
  9.3 1.1 %multiply_convert_fusion.15 = bf16[15,48,128]{2,1,0:T(8,128)(2,1)S(1)} fusion(bf16[15,48,128]{2,1,0:T(8,128)(2,1)} %param.9, f32[15,48]{1,0:T(8,128)S(1)} %add_rsqrt_fusion), kind=kLoop, calls=%fused_computation.120 | loop fusion | flops 276480 | bytes 371520 | tf_op jit(solution)/shard_map/convert_element_type | solution.py:12
  10.4 1.9 %multiply_reduce_fusion.4 = (f32[720]{0:T(1024)S(1)}, f32[720,128]{1,0:T(8,128)S(1)}) fusion(bf16[6,384,128]{2,1,0:T(8,128)(2,1)} %param.12, bf16[720,128]{1,0:T(8,128)(2,1)S(1)} %bitcast.139, f32[384]{0:T(512)S(1)} %get-tuple-element.14, bf16[6,128,384]{2,1,0:T(8,128)(2,1)} %param.10, bf16[720,128]{1,0:T(8,128)(2,1)} %bitcast.136), kind=kOutput, calls=%fused_computation.119 | convolution fusion | flops 144690480 | bytes 938304 | tf_op jit(solution)/shard_map/dot_general | solution.py:18
  12.3 0.9 multiply_reduce_fusion.3
  13.2 0.9 multiply_reduce_fusion.2
  14.1 0.9 multiply_reduce_fusion.1
  15.0 0.9 multiply_reduce_fusion
  15.9 0.8 fusion.4
  16.7 0.2 convolution_convert_fusion.1
  17.0 0.4 copy.36
  17.4 1.4 %reshape.324 = bf16[8,2,5760]{2,1,0:T(2,128)(2,1)} reshape(bf16[128,15,48]{2,1,0:T(8,128)(2,1)S(1)} %bitcast.127) | data formatting | bytes 368640
  18.8 5.2 %all-to-all-start = ((bf16[8,2,5760]{2,1,0:T(2,128)(2,1)}), bf16[8,2,5760]{2,1,0:T(2,128)(2,1)S(1)}, u32[]{:S(2)}, u32[]{:S(2)}) async-start(bf16[8,2,5760]{2,1,0:T(2,128)(2,1)} %reshape.324), calls=%async_computation | async-start | bytes 368640 | tf_op jit(solution)/shard_map/all_to_all | solution.py:64
  24.0 0.0 reduce-scatter.2.cloned.1.call-start
  24.0 0.2 fusion.160
  24.2 5.9 %all-to-all-done = bf16[8,2,5760]{2,1,0:T(2,128)(2,1)S(1)} async-done(((bf16[8,2,5760]{2,1,0:T(2,128)(2,1)}), bf16[8,2,5760]{2,1,0:T(2,128)(2,1)S(1)}, u32[]{:S(2)}, u32[]{:S(2)}) %all-to-all-start) | async-done | bytes 184352 | tf_op jit(solution)/shard_map/all_to_all | solution.py:64
  30.1 0.6 reshape.325
  30.7 0.1 copy.38
  30.8 1.2 %convolution_bitcast_fusion.1 = f32[32,16,2,120]{3,0,2,1:T(8,128)} fusion(bf16[120,48,16,1]{1,2,0,3:T(8,128)(2,1)S(1)} %bitcast.129, f32[32,1,48]{2,0,1:T(8,128)S(1)} %get-tuple-element.17, f32[32,1,48]{2,0,1:T(8,128)S(1)} %get-tuple-element.16), kind=kOutput, calls=%fused_computation.13 | convolution fusion | flops 11805696 | bytes 688128 | tf_op jit(solution)/shard_map/srj,ljk->skrl/dot_general | solution.py:69
  32.1 0.1 dynamic_slice.7
  32.2 0.1 dynamic_slice.6
  32.3 0.2 select_reduce_fusion
  32.4 0.1 fusion.162
  32.5 0.1 multiply_add_fusion
  32.6 20.7 %reduce-scatter.2.cloned.1.call-done = f32[8,16,2,120]{3,0,2,1:T(8,128)} async-done(((f32[32,16,2,120]{3,0,2,1:T(8,128)}), f32[8,16,2,120]{3,0,2,1:T(8,128)}) %reduce-scatter.2.cloned.1.call-update) | async-done | bytes 122896 | tf_op jit(solution)/shard_map/reduce_scatter | solution.py:68
  53.3 0.9 multiply_convert_fusion.16
  54.2 0.2 fusion.6
  54.4 0.1 convolution_convert_fusion.2
  54.5 0.5 copy.41
  55.0 1.0 %reshape.326 = bf16[4,2,3840]{2,1,0:T(2,128)(2,1)} reshape(bf16[120,8,2,16]{3,2,1,0:T(2,128)(2,1)S(1)} %bitcast.131) | data formatting | bytes 122880
  56.0 3.3 %all-to-all-start.1 = ((bf16[4,2,3840]{2,1,0:T(2,128)(2,1)}), bf16[4,2,3840]{2,1,0:T(2,128)(2,1)S(1)}, u32[]{:S(2)}, u32[]{:S(2)}) async-start(bf16[4,2,3840]{2,1,0:T(2,128)(2,1)} %reshape.326), calls=%async_computation.2 | async-start | bytes 122880 | tf_op jit(solution)/shard_map/all_to_all | solution.py:95
  59.3 0.2 fusion.151
  59.5 5.5 %all-to-all-done.1 = bf16[4,2,3840]{2,1,0:T(2,128)(2,1)S(1)} async-done(((bf16[4,2,3840]{2,1,0:T(2,128)(2,1)}), bf16[4,2,3840]{2,1,0:T(2,128)(2,1)S(1)}, u32[]{:S(2)}, u32[]{:S(2)}) %all-to-all-start.1) | async-done | bytes 61472 | tf_op jit(solution)/shard_map/all_to_all | solution.py:95
  65.0 0.4 reshape.327
  65.4 0.9 copy.58
  66.3 0.3 fusion.5
  66.5 0.7 copy.44
  67.2 1.4 %reshape.328 = bf16[4,2,11520]{2,1,0:T(2,128)(2,1)S(1)} reshape(bf16[192,16,30]{2,1,0:T(8,128)(2,1)S(1)} %bitcast.126) | data formatting | bytes 368640
  68.7 9.1 %all_to_all.72 = bf16[4,2,11520]{2,1,0:T(2,128)(2,1)S(1)} all-to-all(bf16[4,2,11520]{2,1,0:T(2,128)(2,1)S(1)} %reshape.328), channel_id=1, replica_groups=mesh['lat'=8,'lon'=4] {'lon'}, dimensions={0} | all-to-all | bytes 368640 | tf_op jit(solution)/shard_map/all_to_all | solution.py:100
  77.8 2.1 %reshape.329 = bf16[192,16,30]{2,1,0:T(8,128)(2,1)S(1)} reshape(bf16[4,2,11520]{2,1,0:T(2,128)(2,1)S(1)} %all_to_all.72) | data formatting | bytes 368640
  79.9 1.3 %copy.57 = bf16[30,4,48,16]{2,1,3,0:T(4,128)(2,1)S(1)} copy(bf16[30,4,48,16]{0,3,2,1:T(8,128)(2,1)S(1)} %bitcast.125) | data formatting | bytes 368640 | tf_op jit(solution)/shard_map/all_to_all | solution.py:100
  81.3 0.1 copy.46
  81.3 1.4 %reshape.330 = bf16[8,2,5760]{2,1,0:T(2,128)(2,1)} reshape(bf16[120,16,48]{2,1,0:T(8,128)(2,1)S(1)} %bitcast.134) | data formatting | bytes 368640
  82.7 3.6 %all-to-all-start.3 = ((bf16[8,2,5760]{2,1,0:T(2,128)(2,1)}), bf16[8,2,5760]{2,1,0:T(2,128)(2,1)S(1)}, u32[]{:S(2)}, u32[]{:S(2)}) async-start(bf16[8,2,5760]{2,1,0:T(2,128)(2,1)} %reshape.330), calls=%async_computation.4 | async-start | bytes 368640 | tf_op jit(solution)/shard_map/all_to_all | solution.py:99
  86.3 0.7 copy.49
  87.0 5.4 %all-to-all-done.3 = bf16[8,2,5760]{2,1,0:T(2,128)(2,1)S(1)} async-done(((bf16[8,2,5760]{2,1,0:T(2,128)(2,1)}), bf16[8,2,5760]{2,1,0:T(2,128)(2,1)S(1)}, u32[]{:S(2)}, u32[]{:S(2)}) %all-to-all-start.3) | async-done | bytes 184352 | tf_op jit(solution)/shard_map/all_to_all | solution.py:99
  92.4 0.5 reshape.331
  92.9 1.0 fusion.3
  (24 shorter events, 0.2 us)
Async XLA Ops:
  7.2 47.0 %copy-start = (bf16[8,120,32]{1,2,0:T(8,128)(2,1)S(1)}, bf16[8,120,32]{1,2,0:T(8,128)(2,1)}, u32[]{:S(2)}) copy-start(bf16[8,120,32]{1,2,0:T(8,128)(2,1)} %param.15) | copy-start | bytes 184324
  10.4 1.9 %copy-start.4 = (bf16[6,384,128]{2,1,0:T(8,128)(2,1)S(1)}, bf16[6,384,128]{2,1,0:T(8,128)(2,1)}, u32[]{:S(2)}) copy-start(bf16[6,384,128]{2,1,0:T(8,128)(2,1)} %param.12) | copy-start | bytes 1769476
  10.4 1.9 %copy-start.5 = (bf16[6,128,384]{2,1,0:T(8,128)(2,1)S(1)}, bf16[6,128,384]{2,1,0:T(8,128)(2,1)}, u32[]{:S(2)}) copy-start(bf16[6,128,384]{2,1,0:T(8,128)(2,1)} %param.10) | copy-start | bytes 1769476
  15.9 0.8 copy-start.2
  17.0 7.1 %copy-start.1 = (s32[32]{0:T(128)S(1)}, s32[32]{0:T(128)}, u32[]{:S(2)}) copy-start(s32[32]{0:T(128)} %param.17) | copy-start | bytes 388
  18.8 11.3 %all-to-all-start = ((bf16[8,2,5760]{2,1,0:T(2,128)(2,1)}), bf16[8,2,5760]{2,1,0:T(2,128)(2,1)S(1)}, u32[]{:S(2)}, u32[]{:S(2)}) async-start(bf16[8,2,5760]{2,1,0:T(2,128)(2,1)} %reshape.324), calls=%async_computation | async-start | bytes 368640 | tf_op jit(solution)/shard_map/all_to_all | solution.py:64
  24.0 29.3 %reduce-scatter.2.cloned.1.call-start = ((), (), s32[]{:S(2)}) async-start(), calls=%async_computation.5 | async-start | bytes 655360 | tf_op jit(solution)/shard_map/reduce_scatter | solution.py:68
  30.8 1.4 %copy-start.6 = (f32[128]{0:T(128)S(1)}, f32[128]{0:T(128)}, u32[]{:S(2)}) copy-start(f32[128]{0:T(128)} %param.14) | copy-start | bytes 1540
  30.8 22.4 %copy-start.3 = (f32[120]{0:T(128)S(1)}, f32[120]{0:T(128)}, u32[]{:S(2)}) copy-start(f32[120]{0:T(128)} %param.13) | copy-start | bytes 1444
  56.0 9.0 %all-to-all-start.1 = ((bf16[4,2,3840]{2,1,0:T(2,128)(2,1)}), bf16[4,2,3840]{2,1,0:T(2,128)(2,1)S(1)}, u32[]{:S(2)}, u32[]{:S(2)}) async-start(bf16[4,2,3840]{2,1,0:T(2,128)(2,1)} %reshape.326), calls=%async_computation.2 | async-start | bytes 122880 | tf_op jit(solution)/shard_map/all_to_all | solution.py:95
  82.7 9.7 %all-to-all-start.3 = ((bf16[8,2,5760]{2,1,0:T(2,128)(2,1)}), bf16[8,2,5760]{2,1,0:T(2,128)(2,1)S(1)}, u32[]{:S(2)}, u32[]{:S(2)}) async-start(bf16[8,2,5760]{2,1,0:T(2,128)(2,1)} %reshape.330), calls=%async_computation.4 | async-start | bytes 368640 | tf_op jit(solution)/shard_map/all_to_all | solution.py:99
Sparse Core Ops, SparseCore 0:
  32.2 20.9 reduce-scatter.1
where the time goes:
time: 101 us
  waiting for transfers between devices  37.4 us (37%)
  local copies, waits for them, and re-layouts  14.7 us (15%)
  between operations  14.3 us (14%)
  starting transfers between devices  12.1 us (12%)
  matrix products  9.23 us (9%)
  blocking collectives  9.13 us (9%)
  other arithmetic  3.88 us (4%)
    reduce_scatter x1, waiting for transfers between devices, local(): lax.psum_scatter(jnp.einsum('srj,ljk->skrl', trig_rows, levels, preferred...  20.7 us
    unnamed x23, local copies, waits for them, and re-layouts  9.62 us
    all_to_all x1, blocking collectives, local(): lax.all_to_all(band_tendency, 'lon', split_axis=1, concat_axis=0, tiled=T...  9.13 us
    dot_general x6, matrix products, column_layers(): jnp.dot(activation, weight_out[layer_idx], preferred_element_type=jnp.flo...  6.23 us
    all_to_all x1, waiting for transfers between devices, local(): lax.all_to_all(ordered, 'lat', split_axis=2, concat_axis=0, tiled=True)  5.87 us
    all_to_all x1, waiting for transfers between devices, local(): lax.all_to_all(back_fourier, 'lon', split_axis=3, concat_axis=0, tiled=True)  5.47 us
    all_to_all x1, waiting for transfers between devices, local(): lax.all_to_all(lax.all_to_all(band_tendency, 'lon', split_axis=1, concat_...  5.38 us
    all_to_all x1, starting transfers between devices, local(): lax.all_to_all(ordered, 'lat', split_axis=2, concat_axis=0, tiled=True)  5.18 us
  transfers between devices with their start and end apart: 4, of which 4 were waited for; matrix products, arithmetic and copies ran while one was open for 2% of the time, Pallas kernels for 0%

commit v1 on v0

--- a/solution.py
+++ b/solution.py
@@ -3,6 +3,28 @@
 import jax.numpy as jnp
 from jax import lax
 from jax.sharding import PartitionSpec as P
+
+
+def serve_hubs_by_axis(original, axis_name):
+    r2 = lax.axis_size(axis_name)
+    a_now = lax.axis_index(axis_name)
+    oldest, row_out = (r2, a_now)
+    all_values = list(original.shape)
+    reply = original.shape[1] // oldest
+    all_values[1] = reply
+    after = all_values[0]
+    all_values[0] = after * oldest
+    current_block = jnp.zeros(all_values, original.dtype)
+    for i0 in range(oldest):
+        found_now = lax.dynamic_slice_in_dim(original, (row_out ^ i0) * reply, reply, axis=1)
+        if i0:
+            t_next = range(oldest)
+            block_out = map(lambda b: (b, b ^ i0), t_next)
+            found_now = lax.ppermute(found_now, axis_name, list(block_out))
+        current_block = lax.dynamic_update_slice_in_dim(
+            current_block, found_now, (row_out ^ i0) * after, axis=0
+        )
+    return current_block
 
 
 def column_layers(column_rows, weight_in, bias_in, weight_out):
@@ -97,11 +119,7 @@
         "skrl,srj->ljk", all_waves, trig_all, preferred_element_type=jnp.float32
     ).astype(jnp.bfloat16)
     tendency = lax.all_to_all(
-        lax.all_to_all(band_tendency, "lon", split_axis=1, concat_axis=0, tiled=True),
-        "lat",
-        split_axis=0,
-        concat_axis=2,
-        tiled=True,
+        serve_hubs_by_axis(band_tendency, "lon"), "lat", split_axis=0, concat_axis=2, tiled=True
     )
     tendency = pick_channels(tendency, chosen.T)
     updated = (columns.astype(jnp.float32) + tendency.astype(jnp.float32)).astype(jnp.bfloat16)

time: 101 us -> 98 us (0.970)
  blocking collectives: 9.13 us -> 0 us
  waiting for transfers between devices: 37.4 us -> 43.9 us
  local copies, waits for them, and re-layouts: 14.7 us -> 9.73 us
  starting transfers between devices: 12.1 us -> 16.3 us
    all_to_all x1 -> x0, blocking collectives: 9.13 us -> none  [local(): lax.all_to_all(band_tendency, 'lon', split_axis=1, concat_axis=0, tiled=T...]
    ppermute x0 -> x3, waiting for transfers between devices: none -> 6.63 us  [serve_hubs_by_axis(): found_now = lax.ppermute(found_now, axis_name, list(block_out))]
    ppermute x0 -> x3, starting transfers between devices: none -> 4.45 us  [serve_hubs_by_axis(): found_now = lax.ppermute(found_now, axis_name, list(block_out))]
    unnamed x23, local copies, waits for them, and re-layouts: 9.62 us -> 6.07 us
    all_to_all x3 -> x1, local copies, waits for them, and re-layouts: 1.42 us -> 0.04 us  [local(): lax.all_to_all(serve_hubs_by_axis(band_tendency, 'lon'), 'lat', split_axi...]
  transfers between devices with their start and end apart: 4 -> 7, of which waited for: 4 -> 6; matrix products, arithmetic and copies ran while one was open for 2% -> 2% of each run, Pallas kernels for 0% -> 0%
where the time goes in v1:
time: 98 us; the launch traced here: 97.4 us
  waiting for transfers between devices  43.9 us (45%)
  starting transfers between devices  16.3 us (17%)
  between operations  14.4 us (15%)
  local copies, waits for them, and re-layouts  9.73 us (10%)
  matrix products  9.16 us (9%)
  other arithmetic  3.92 us (4%)
    reduce_scatter x1, waiting for transfers between devices, local(): lax.psum_scatter(jnp.einsum('srj,ljk->skrl', trig_rows, levels, preferred...  20.7 us
    ppermute x3, waiting for transfers between devices, serve_hubs_by_axis(): found_now = lax.ppermute(found_now, axis_name, list(block_out))  6.63 us
    dot_general x6, matrix products, column_layers(): jnp.dot(activation, weight_out[layer_idx], preferred_element_type=jnp.flo...  6.15 us
    unnamed x23, local copies, waits for them, and re-layouts  6.07 us
    all_to_all x1, waiting for transfers between devices, local(): lax.all_to_all(ordered, 'lat', split_axis=2, concat_axis=0, tiled=True)  5.87 us
    all_to_all x1, waiting for transfers between devices, local(): lax.all_to_all(back_fourier, 'lon', split_axis=3, concat_axis=0, tiled=True)  5.44 us
    all_to_all x1, waiting for transfers between devices, local(): lax.all_to_all(serve_hubs_by_axis(band_tendency, 'lon'), 'lat', split_axi...  5.31 us
    all_to_all x1, starting transfers between devices, local(): lax.all_to_all(ordered, 'lat', split_axis=2, concat_axis=0, tiled=True)  5.18 us
  transfers between devices with their start and end apart: 7, of which 6 were waited for; matrix products, arithmetic and copies ran while one was open for 2% of the time, Pallas kernels for 0%

profile of v1, /device:TPU:0, one launch (start us, length us, event | category | flops | bytes accessed | tf_op | source)
XLA Modules:
  0.0 97.4 jit_solution(12486780858339281129)
XLA Ops:
  7.2 1.2 %multiply_reduce_fusion.5 = f32[15,48]{1,0:T(8,128)S(1)} fusion(bf16[15,48,128]{2,1,0:T(8,128)(2,1)} %param.9), kind=kLoop, calls=%fused_computation.120 | loop fusion | flops 275760 | bytes 187200 | tf_op jit(solution)/shard_map/reduce_sum | solution.py:33
  8.4 1.0 slice_reduce_fusion
  9.3 1.1 %multiply_convert_fusion.15 = bf16[15,48,128]{2,1,0:T(8,128)(2,1)S(1)} fusion(bf16[15,48,128]{2,1,0:T(8,128)(2,1)} %param.9, f32[15,48]{1,0:T(8,128)S(1)} %add_rsqrt_fusion), kind=kLoop, calls=%fused_computation.119 | loop fusion | flops 276480 | bytes 371520 | tf_op jit(solution)/shard_map/convert_element_type | solution.py:34
  10.4 1.8 %multiply_reduce_fusion.4 = (f32[720]{0:T(1024)S(1)}, f32[720,128]{1,0:T(8,128)S(1)}) fusion(bf16[6,384,128]{2,1,0:T(8,128)(2,1)} %param.12, bf16[720,128]{1,0:T(8,128)(2,1)S(1)} %bitcast.135, f32[384]{0:T(512)S(1)} %get-tuple-element.14, bf16[6,128,384]{2,1,0:T(8,128)(2,1)} %param.10, bf16[720,128]{1,0:T(8,128)(2,1)S(1)} %bitcast.132), kind=kOutput, calls=%fused_computation.118 | convolution fusion | flops 144690480 | bytes 938304 | tf_op jit(solution)/shard_map/dot_general | solution.py:40
  12.3 0.9 multiply_reduce_fusion.3
  13.2 0.9 multiply_reduce_fusion.2
  14.1 0.9 multiply_reduce_fusion.1
  15.0 0.9 multiply_reduce_fusion
  15.9 0.8 fusion.4
  16.7 0.2 convolution_convert_fusion.1
  16.9 0.4 copy.39
  17.4 1.4 %reshape.324 = bf16[8,2,5760]{2,1,0:T(2,128)(2,1)} reshape(bf16[128,15,48]{2,1,0:T(8,128)(2,1)S(1)} %bitcast.124) | data formatting | bytes 368640
  18.8 5.2 %all-to-all-start = ((bf16[8,2,5760]{2,1,0:T(2,128)(2,1)}), bf16[8,2,5760]{2,1,0:T(2,128)(2,1)S(1)}, u32[]{:S(2)}, u32[]{:S(2)}) async-start(bf16[8,2,5760]{2,1,0:T(2,128)(2,1)} %reshape.324), calls=%async_computation | async-start | bytes 368640 | tf_op jit(solution)/shard_map/all_to_all | solution.py:86
  24.0 0.2 fusion.159
  24.2 5.9 %all-to-all-done = bf16[8,2,5760]{2,1,0:T(2,128)(2,1)S(1)} async-done(((bf16[8,2,5760]{2,1,0:T(2,128)(2,1)}), bf16[8,2,5760]{2,1,0:T(2,128)(2,1)S(1)}, u32[]{:S(2)}, u32[]{:S(2)}) %all-to-all-start) | async-done | bytes 184352 | tf_op jit(solution)/shard_map/all_to_all | solution.py:86
  30.1 0.6 reshape.325
  30.7 0.1 copy.41
  30.8 1.2 %convolution_bitcast_fusion.1 = f32[32,16,2,120]{3,0,2,1:T(8,128)} fusion(bf16[120,48,16,1]{1,2,0,3:T(8,128)(2,1)S(1)} %bitcast.126, f32[32,1,48]{2,0,1:T(8,128)S(1)} %get-tuple-element.21, f32[32,1,48]{2,0,1:T(8,128)S(1)} %get-tuple-element.20), kind=kOutput, calls=%fused_computation.13 | convolution fusion | flops 11805696 | bytes 688128 | tf_op jit(solution)/shard_map/srj,ljk->skrl/dot_general | solution.py:91
  32.1 0.1 dynamic_slice.19
  32.2 0.1 dynamic_slice.18
  32.2 0.2 select_reduce_fusion
  32.4 0.1 fusion.161
  32.5 0.1 multiply_add_fusion
  32.6 20.7 %reduce-scatter.2.cloned.1.call-done = f32[8,16,2,120]{3,0,2,1:T(8,128)} async-done(((f32[32,16,2,120]{3,0,2,1:T(8,128)}), f32[8,16,2,120]{3,0,2,1:T(8,128)}) %reduce-scatter.2.cloned.1.call-update) | async-done | bytes 122896 | tf_op jit(solution)/shard_map/reduce_scatter | solution.py:90
  53.2 0.9 multiply_convert_fusion.16
  54.2 0.2 fusion.5
  54.3 0.1 convolution_convert_fusion.2
  54.5 0.5 copy.44
  54.9 1.0 %reshape.326 = bf16[4,2,3840]{2,1,0:T(2,128)(2,1)} reshape(bf16[120,8,2,16]{3,2,1,0:T(2,128)(2,1)S(1)} %bitcast.129) | data formatting | bytes 122880
  56.0 3.3 %all-to-all-start.1 = ((bf16[4,2,3840]{2,1,0:T(2,128)(2,1)}), bf16[4,2,3840]{2,1,0:T(2,128)(2,1)S(1)}, u32[]{:S(2)}, u32[]{:S(2)}) async-start(bf16[4,2,3840]{2,1,0:T(2,128)(2,1)} %reshape.326), calls=%async_computation.2 | async-start | bytes 122880 | tf_op jit(solution)/shard_map/all_to_all | solution.py:117
  59.3 0.2 fusion.150
  59.5 5.4 %all-to-all-done.1 = bf16[4,2,3840]{2,1,0:T(2,128)(2,1)S(1)} async-done(((bf16[4,2,3840]{2,1,0:T(2,128)(2,1)}), bf16[4,2,3840]{2,1,0:T(2,128)(2,1)S(1)}, u32[]{:S(2)}, u32[]{:S(2)}) %all-to-all-start.1) | async-done | bytes 61472 | tf_op jit(solution)/shard_map/all_to_all | solution.py:117
  65.0 0.4 reshape.327
  65.4 0.9 copy.61
  66.2 0.3 fusion
  66.5 0.3 dynamic-slice_bitcast_fusion
  66.8 0.8 collective-permute-start.2
  67.6 1.6 %collective-permute-start.1 = (bf16[30,48,16]{1,0,2:T(8,128)(2,1)S(1)}, bf16[30,48,16]{1,0,2:T(8,128)(2,1)S(1)}, u32[]{:S(2)}, u32[]{:S(2)}) collective-permute-start(bf16[30,48,16]{1,0,2:T(8,128)(2,1)S(1)} %get-tuple-element.17), channel_id=1, source_target_pairs={{0,2},{1,3},{2,0},{3,1},{4,6},{5,7},{6,4},{7,5},{8,10},{9,11},{10,... | collective-permute-start | bytes 138248 | tf_op jit(solution)/shard_map/ppermute | solution.py:23
  69.2 2.0 %collective-permute-start = (bf16[30,48,16]{1,0,2:T(8,128)(2,1)S(1)}, bf16[30,48,16]{1,0,2:T(8,128)(2,1)S(1)}, u32[]{:S(2)}, u32[]{:S(2)}) collective-permute-start(bf16[30,48,16]{1,0,2:T(8,128)(2,1)S(1)} %get-tuple-element.18), channel_id=1, source_target_pairs={{0,1},{1,0},{2,3},{3,2},{4,5},{5,4},{6,7},{7,6},{8,9},{9,8},{10,11... | collective-permute-start | bytes 138248 | tf_op jit(solution)/shard_map/ppermute | solution.py:23
  71.3 0.1 copy_dynamic-update-slice_fusion.3
  71.4 4.0 %collective-permute-done = bf16[30,48,16]{1,0,2:T(8,128)(2,1)S(1)} collective-permute-done((bf16[30,48,16]{1,0,2:T(8,128)(2,1)S(1)}, bf16[30,48,16]{1,0,2:T(8,128)(2,1)S(1)}, u32[]{:S(2)}, u32[]{:S(2)}) %collective-permute-start) | collective-permute-done | bytes 46112 | tf_op jit(solution)/shard_map/ppermute | solution.py:23
  75.5 2.6 %collective-permute-done.1 = bf16[30,48,16]{1,0,2:T(8,128)(2,1)S(1)} collective-permute-done((bf16[30,48,16]{1,0,2:T(8,128)(2,1)S(1)}, bf16[30,48,16]{1,0,2:T(8,128)(2,1)S(1)}, u32[]{:S(2)}, u32[]{:S(2)}) %collective-permute-start.1) | collective-permute-done | bytes 46112 | tf_op jit(solution)/shard_map/ppermute | solution.py:23
  78.2 1.4 %reshape.328 = bf16[8,2,5760]{2,1,0:T(2,128)(2,1)} reshape(bf16[120,16,48]{2,1,0:T(8,128)(2,1)S(1)} %bitcast.127) | data formatting | bytes 368640
  79.6 3.4 %all-to-all-start.2 = ((bf16[8,2,5760]{2,1,0:T(2,128)(2,1)}), bf16[8,2,5760]{2,1,0:T(2,128)(2,1)S(1)}, u32[]{:S(2)}, u32[]{:S(2)}) async-start(bf16[8,2,5760]{2,1,0:T(2,128)(2,1)} %reshape.328), calls=%async_computation.3 | async-start | bytes 368640 | tf_op jit(solution)/shard_map/all_to_all | solution.py:121
  83.0 0.7 copy.53
  83.7 5.3 %all-to-all-done.2 = bf16[8,2,5760]{2,1,0:T(2,128)(2,1)S(1)} async-done(((bf16[8,2,5760]{2,1,0:T(2,128)(2,1)}), bf16[8,2,5760]{2,1,0:T(2,128)(2,1)S(1)}, u32[]{:S(2)}, u32[]{:S(2)}) %all-to-all-start.2) | async-done | bytes 184352 | tf_op jit(solution)/shard_map/all_to_all | solution.py:121
  89.0 0.5 reshape.329
  89.6 1.0 %fusion.3 = bf16[15,48,128]{2,1,0:T(8,128)(2,1)} fusion(bf16[15,48,128]{1,2,0:T(8,128)(2,1)S(1)} %bitcast.128, bf16[15,48,128]{2,1,0:T(8,128)(2,1)S(1)} %bitcast.134, s32[128]{0:T(128)S(1)} %copy-done.3), kind=kOutput, calls=%fused_computation.25 | convolution fusion | flops 24070144 | bytes 553472 | tf_op jit(solution)/shard_map/ljc,ck->ljk/dot_general | solution.py:57
  (32 shorter events, 0.5 us)
Async XLA Ops:
  7.2 47.0 %copy-start = (bf16[8,120,32]{1,2,0:T(8,128)(2,1)S(1)}, bf16[8,120,32]{1,2,0:T(8,128)(2,1)}, u32[]{:S(2)}) copy-start(bf16[8,120,32]{1,2,0:T(8,128)(2,1)} %param.15) | copy-start | bytes 184324
  7.2 3.2 %copy-start.1 = (bf16[15,48,128]{2,1,0:T(8,128)(2,1)S(1)}, bf16[15,48,128]{2,1,0:T(8,128)(2,1)}, u32[]{:S(2)}) copy-start(bf16[15,48,128]{2,1,0:T(8,128)(2,1)} %param.9) | copy-start | bytes 552964
  10.4 1.9 %copy-start.5 = (bf16[6,384,128]{2,1,0:T(8,128)(2,1)S(1)}, bf16[6,384,128]{2,1,0:T(8,128)(2,1)}, u32[]{:S(2)}) copy-start(bf16[6,384,128]{2,1,0:T(8,128)(2,1)} %param.12) | copy-start | bytes 1769476
  10.4 1.9 %copy-start.6 = (bf16[6,128,384]{2,1,0:T(8,128)(2,1)S(1)}, bf16[6,128,384]{2,1,0:T(8,128)(2,1)}, u32[]{:S(2)}) copy-start(bf16[6,128,384]{2,1,0:T(8,128)(2,1)} %param.10) | copy-start | bytes 1769476
  15.9 0.8 copy-start.3
  17.4 6.6 %copy-start.2 = (s32[32]{0:T(128)S(1)}, s32[32]{0:T(128)}, u32[]{:S(2)}) copy-start(s32[32]{0:T(128)} %param.17) | copy-start | bytes 388
  18.8 11.3 %all-to-all-start = ((bf16[8,2,5760]{2,1,0:T(2,128)(2,1)}), bf16[8,2,5760]{2,1,0:T(2,128)(2,1)S(1)}, u32[]{:S(2)}, u32[]{:S(2)}) async-start(bf16[8,2,5760]{2,1,0:T(2,128)(2,1)} %reshape.324), calls=%async_computation | async-start | bytes 368640 | tf_op jit(solution)/shard_map/all_to_all | solution.py:86
  23.9 29.3 %reduce-scatter.2.cloned.1.call-start = ((), (), s32[]{:S(2)}) async-start(), calls=%async_computation.4 | async-start | bytes 655360 | tf_op jit(solution)/shard_map/reduce_scatter | solution.py:90
  30.8 1.4 %copy-start.7 = (f32[128]{0:T(128)S(1)}, f32[128]{0:T(128)}, u32[]{:S(2)}) copy-start(f32[128]{0:T(128)} %param.14) | copy-start | bytes 1540
  30.8 22.4 %copy-start.4 = (f32[120]{0:T(128)S(1)}, f32[120]{0:T(128)}, u32[]{:S(2)}) copy-start(f32[120]{0:T(128)} %param.13) | copy-start | bytes 1444
  56.0 9.0 %all-to-all-start.1 = ((bf16[4,2,3840]{2,1,0:T(2,128)(2,1)}), bf16[4,2,3840]{2,1,0:T(2,128)(2,1)S(1)}, u32[]{:S(2)}, u32[]{:S(2)}) async-start(bf16[4,2,3840]{2,1,0:T(2,128)(2,1)} %reshape.326), calls=%async_computation.2 | async-start | bytes 122880 | tf_op jit(solution)/shard_map/all_to_all | solution.py:117
  66.8 11.4 %collective-permute-start.2 = (bf16[30,48,16]{1,0,2:T(8,128)(2,1)S(1)}, bf16[30,48,16]{1,0,2:T(8,128)(2,1)S(1)}, u32[]{:S(2)}, u32[]{:S(2)}) collective-permute-start(bf16[30,48,16]{1,0,2:T(8,128)(2,1)S(1)} %get-tuple-element.16), channel_id=1, source_target_pairs={{0,3},{1,2},{2,1},{3,0},{4,7},{5,6},{6,5},{7,4},{8,11},{9,10},{10,... | collective-permute-start | bytes 138248 | tf_op jit(solution)/shard_map/ppermute | solution.py:23
  67.6 10.5 %collective-permute-start.1 = (bf16[30,48,16]{1,0,2:T(8,128)(2,1)S(1)}, bf16[30,48,16]{1,0,2:T(8,128)(2,1)S(1)}, u32[]{:S(2)}, u32[]{:S(2)}) collective-permute-start(bf16[30,48,16]{1,0,2:T(8,128)(2,1)S(1)} %get-tuple-element.17), channel_id=1, source_target_pairs={{0,2},{1,3},{2,0},{3,1},{4,6},{5,7},{6,4},{7,5},{8,10},{9,11},{10,... | collective-permute-start | bytes 138248 | tf_op jit(solution)/shard_map/ppermute | solution.py:23
  69.2 6.2 %collective-permute-start = (bf16[30,48,16]{1,0,2:T(8,128)(2,1)S(1)}, bf16[30,48,16]{1,0,2:T(8,128)(2,1)S(1)}, u32[]{:S(2)}, u32[]{:S(2)}) collective-permute-start(bf16[30,48,16]{1,0,2:T(8,128)(2,1)S(1)} %get-tuple-element.18), channel_id=1, source_target_pairs={{0,1},{1,0},{2,3},{3,2},{4,5},{5,4},{6,7},{7,6},{8,9},{9,8},{10,11... | collective-permute-start | bytes 138248 | tf_op jit(solution)/shard_map/ppermute | solution.py:23
  79.6 9.4 %all-to-all-start.2 = ((bf16[8,2,5760]{2,1,0:T(2,128)(2,1)}), bf16[8,2,5760]{2,1,0:T(2,128)(2,1)S(1)}, u32[]{:S(2)}, u32[]{:S(2)}) async-start(bf16[8,2,5760]{2,1,0:T(2,128)(2,1)} %reshape.328), calls=%async_computation.3 | async-start | bytes 368640 | tf_op jit(solution)/shard_map/all_to_all | solution.py:121
Sparse Core Ops, SparseCore 0:
  32.2 20.9 reduce-scatter.1
